TPU v7x, 128 devices: a whole 4x4x4 slice. The times are simulated.
128 devices in a mesh: row: 16 (over z, y_hi, core), col: 8 (over x, y_lo).
Axes of the slice: x: 4, y: 4 (y_hi: 2, y_lo: 2; y = y_hi * 2 + y_lo), z: 4, core: 2. Of those that a mesh axis runs over, the one named last changes fastest.
Arguments:
- roll_hidden: bfloat16 [5376, 4096], P(('row', 'col')), may hold values from -6 to 6
- roll_cotangent: bfloat16 [5376, 4096], P(('row', 'col')), may hold values from -6 to 6
- lengths: int32 [128], P(('row', 'col')), may hold values from 1 to 42, as said below
- owners: int32 [128], P(('row', 'col')), may hold values from 0 to 15, as said below
- prompts: int32 [128], P(('row', 'col')), may hold values from 0 to 15
- rewards: float32 [128], P(('row', 'col')), may hold values from -5 to 5
- gate_weight: bfloat16 [4096, 14784], P('col', 'row'), may hold values from -0.09375 to 0.09375
- up_weight: bfloat16 [4096, 14784], P('col', 'row'), may hold values from -0.09375 to 0.09375
- down_weight: bfloat16 [14784, 4096], P('row', 'col'), may hold values from -0.046875 to 0.046875
Outputs:
- grad_input: bfloat16 [2048, 4096], P('row', 'col')
- grad_gate: bfloat16 [4096, 14784], P('col', 'row')
- grad_up: bfloat16 [4096, 14784], P('col', 'row')
- grad_down: bfloat16 [14784, 4096], P('row', 'col')
Inputs may be any that keep to these rules, and one draw needn't show every extreme that they name: `owners`: each owner value names exactly 8 rows; the lengths of one owner's rows sum to at most 128, and to exactly 128 for some owner in every draw. `lengths`: some row has length 42 in every draw.
All inputs are finite; a program needn't handle non-finite values.
Results may differ from a plain program's by a relative error of at most 0.025.
Values may be sent and summed in bfloat16 or wider, within the bound.
No kernel may reach another device: no remote copies, remote signals or barrier semaphores. Data moves between devices by JAX's collectives and lax.ppermute only.
A program may use at most 128 MiB of HBM per device.

v0:
```python
import jax
import jax.numpy as jnp
from jax import lax
from jax.sharding import PartitionSpec as P

CAPR = 128
spread_floor = 0.7


def in_one_piece(arrays, axis, split_dim, concat_dim, along):
    ends, at = ([], 0)
    for a in arrays[:-1]:
        at += a.shape[along]
        ends.append(at)
    both = jnp.concatenate(arrays, axis=along)
    return tuple(
        jnp.split(
            lax.all_to_all(both, axis, split_axis=split_dim, concat_axis=concat_dim, tiled=True),
            ends,
            axis=along,
        )
    )


def sent_together(arrays, axis, dim, along):
    widths = [a.shape[along] for a in arrays]
    both = jnp.concatenate(arrays, axis=along)
    result = lax.all_gather(both, axis, axis=dim, tiled=True)
    return tuple(jnp.split(result, [sum(widths[:k]) for k in range(1, len(widths))], axis=along))


def cut_along(array, dim, size):
    lengths = array.shape
    tiles = array.reshape(*lengths[:dim], size, lengths[dim] // size, *lengths[dim + 1 :])
    return jnp.moveaxis(tiles, dim, 0)


def sent_and_summed(array, axis, dim):
    size = lax.axis_size(axis)
    tiles = lax.all_to_all(cut_along(array, dim, size), axis, 0, 0, tiled=True)
    return jnp.sum(tiles.astype(jnp.float32), axis=0)


def row_weights(lengths, prompts, rewards, count_prompts):
    onehot = (prompts[:, None] == jnp.arange(count_prompts, dtype=jnp.int32)[None, :]).astype(
        jnp.float32
    )
    counts = jnp.maximum(jnp.sum(onehot, 0), 1.0)
    means = jnp.sum(onehot * rewards[:, None], 0) / counts
    centred = rewards - jnp.sum(onehot * means[None, :], 1)
    spreads = jnp.sqrt(jnp.sum(onehot * (centred * centred)[:, None], 0) / counts)
    divisor = jnp.maximum(jnp.sum(onehot * spreads[None, :], 1), spread_floor)
    return centred / divisor / lengths.astype(jnp.float32)


def row_offsets(lengths, owners):
    count = lengths.shape[0]
    places = jnp.arange(count, dtype=jnp.int32)
    earlier = (owners[None, :] == owners[:, None]) & (places[None, :] < places[:, None])
    return jnp.sum(jnp.where(earlier, lengths[None, :], 0), 1)


def source_index(lengths, owners, offsets, slot_count, capacity, total):
    count = lengths.shape[0]
    slots = jnp.arange(slot_count, dtype=jnp.int32)
    live = slots[None, :] < lengths[:, None]
    target = jnp.where(live, owners[:, None] * capacity + offsets[:, None] + slots[None, :], total)
    flat_source = slots[None, :] * count + jnp.arange(count, dtype=jnp.int32)[:, None]
    empty = jnp.full((total,), slot_count * count, jnp.int32)
    return empty.at[target.reshape(-1)].set(flat_source.reshape(-1), mode="drop")


def per_device(
    roll_hidden,
    roll_cotangent,
    lengths,
    owners,
    prompts,
    rewards,
    gate_weight,
    up_weight,
    down_weight,
):
    row_count = lax.axis_size("row")
    col_count = lax.axis_size("col")
    total_tokens = row_count * CAPR
    count_prompts = row_count * col_count // 8
    slot_count = roll_hidden.shape[0]
    width = roll_hidden.shape[1] // col_count
    local = jnp.stack(
        [
            lengths.astype(jnp.float32),
            owners.astype(jnp.float32),
            prompts.astype(jnp.float32),
            rewards,
        ],
        axis=1,
    )
    table = lax.all_gather(local, ("row", "col"), axis=0, tiled=True)
    all_lengths = table[:, 0].astype(jnp.int32)
    all_owners = table[:, 1].astype(jnp.int32)
    all_prompts = table[:, 2].astype(jnp.int32)
    weights = row_weights(all_lengths, all_prompts, table[:, 3], count_prompts)
    offsets = row_offsets(all_lengths, all_owners)
    mine = lax.dynamic_slice_in_dim(weights, lax.axis_index(("row", "col")), 1, 0)
    live = (jnp.arange(slot_count, dtype=jnp.int32) < lengths[0])[:, None]
    upstream = jnp.where(live, roll_cotangent.astype(jnp.float32) * mine[0], 0.0).astype(
        jnp.bfloat16
    )
    hidden_blocks = roll_hidden.reshape(slot_count, col_count, width)
    upstream_blocks = upstream.reshape(slot_count, col_count, width)
    hidden_cols, upstream_cols = in_one_piece((hidden_blocks, upstream_blocks), "col", 1, 1, 0)
    hidden_all, upstream_all = sent_together((hidden_cols, upstream_cols), "row", 1, 0)
    sources = source_index(all_lengths, all_owners, offsets, slot_count, CAPR, total_tokens)
    packed = jnp.take(hidden_all.reshape(-1, width), sources, axis=0, mode="fill", fill_value=0)
    packed_grad = jnp.take(
        upstream_all.reshape(-1, width), sources, axis=0, mode="fill", fill_value=0
    )
    gate_term = jnp.dot(packed, gate_weight, preferred_element_type=jnp.float32)
    up_term = jnp.dot(packed, up_weight, preferred_element_type=jnp.float32)
    gate, upval = (
        lax.psum(gate_term.astype(jnp.bfloat16), "col").astype(jnp.float32),
        lax.psum(up_term.astype(jnp.bfloat16), "col").astype(jnp.float32),
    )
    sig = jax.nn.sigmoid(gate)
    silu = gate * sig
    hidden = (silu * upval).astype(jnp.bfloat16)
    contract_cols = (((1,), (1,)), ((), ()))
    grad_term = lax.dot_general(
        packed_grad, down_weight, contract_cols, preferred_element_type=jnp.float32
    )
    grad_hidden = lax.psum(grad_term.astype(jnp.bfloat16), "col").astype(jnp.float32)
    grad_gate_act = (grad_hidden * upval * sig * (1.0 + gate * (1.0 - sig))).astype(jnp.bfloat16)
    grad_up_act = (grad_hidden * silu).astype(jnp.bfloat16)
    contract_rows = (((0,), (0,)), ((), ()))
    grad_down = lax.dot_general(
        hidden, packed_grad, contract_rows, preferred_element_type=jnp.float32
    ).astype(jnp.bfloat16)
    grad_gate = lax.dot_general(
        packed, grad_gate_act, contract_rows, preferred_element_type=jnp.float32
    ).astype(jnp.bfloat16)
    grad_up = lax.dot_general(
        packed, grad_up_act, contract_rows, preferred_element_type=jnp.float32
    ).astype(jnp.bfloat16)
    term = lax.dot_general(
        grad_gate_act, gate_weight, contract_cols, preferred_element_type=jnp.float32
    )
    grad_input = sent_and_summed(
        (
            term
            + lax.dot_general(
                grad_up_act, up_weight, contract_cols, preferred_element_type=jnp.float32
            )
        ).astype(jnp.bfloat16),
        "row",
        0,
    )
    return (grad_input.astype(jnp.bfloat16), grad_gate, grad_up, grad_down)


def solution(mesh):
    return jax.shard_map(
        per_device,
        mesh=mesh,
        in_specs=(
            P(("row", "col"), None),
            P(("row", "col"), None),
            P(("row", "col")),
            P(("row", "col")),
            P(("row", "col")),
            P(("row", "col")),
            P("col", "row"),
            P("col", "row"),
            P("row", "col"),
        ),
        out_specs=(P("row", "col"), P("col", "row"), P("col", "row"), P("row", "col")),
        check_vma=False,
    )
```

profile of v0, /device:TPU:4, one launch (start us, length us, event | category | flops | bytes accessed | tf_op | source)
XLA Modules:
  0.0 991.0 jit_solution(10023484400698001869)
XLA Ops:
  10.0 307.3 %all-gather = f32[128,1,4]{2,1,0:T(1,128)S(1)} all-gather(f32[1,1,4]{2,1,0:T(1,128)S(1)} %maximum_bitcast_fusion), channel_id=1, replica_groups=mesh['row'=16,'col'=8] {'row','col'}, dimensions={0}, use_global_device_ids=true | all-gather | bytes 2064 | tf_op jit(solution)/shard_map/all_gather | solution.py:99
  317.8 0.6 dynamic_slice.3
  318.4 1.8 select_convert_fusion
  320.3 1.1 copy.30
  321.8 19.5 %all_to_all.10 = bf16[84,8,512]{2,0,1:T(8,128)(2,1)S(1)} all-to-all(bf16[84,8,512]{2,0,1:T(8,128)(2,1)S(1)} %copy.28), channel_id=1, replica_groups=mesh['row'=16,'col'=8] {'col'}, dimensions={1} | all-to-all | bytes 1376256 | tf_op jit(solution)/shard_map/all_to_all | solution.py:18
  341.3 1.1 copy.29
  343.1 20.4 %scatter_custom_fusion = s32[2048]{0:T(1024)S(1)} fusion(s32[5376]{0:T(1024)S(1)} %fusion.15, s32[5376]{0:T(1024)S(1)} %reshape.149, s32[]{:T(128)} %constant.19.clone.1), kind=kCustom, calls=%fused_computation.47 | custom fusion | bytes 8196 | tf_op jit(solution)/shard_map/scatter | solution.py:70
  363.5 65.8 %all-gather.3.cloned.1.call-done = bf16[84,128,512]{2,1,0:T(8,128)(2,1)} async-done(((bf16[84,8,512]{2,1,0:T(8,128)(2,1)}), bf16[84,128,512]{2,1,0:T(8,128)(2,1)}) %all-gather.3.cloned.1.call-update) | async-done | bytes 11010064 | tf_op jit(solution)/shard_map/all_gather | solution.py:28
  429.3 9.6 fusion.25
  438.9 10.9 %gather_fusion = bf16[2048,512]{1,0:T(8,128)(2,1)S(1)} fusion(bf16[5376,512]{1,0:T(8,128)(2,1)} %bitcast.57, s32[2048]{0:T(1024)S(1)} %fusion.16), kind=kCustom, calls=%fused_computation.clone | custom fusion | bytes 4202496 | tf_op jit(solution)/shard_map/jit(_take)/gather | solution.py:116
  449.8 13.2 %gather_fusion.1 = bf16[2048,512]{1,0:T(8,128)(2,1)} fusion(bf16[5376,512]{1,0:T(8,128)(2,1)} %bitcast.56, s32[2048]{0:T(1024)S(1)} %fusion.16), kind=kCustom, calls=%fused_computation.1.clone | custom fusion | bytes 4202496 | tf_op jit(solution)/shard_map/jit(_take)/gather | solution.py:115
  463.0 5.9 convolution_convert_fusion
  468.9 3.9 convolution_convert_fusion.1
  472.8 3.9 convolution_convert_fusion.2
  476.7 455.9 %all-reduce.3.cloned.1.call-done = (bf16[2048,924]{0,1:T(8,128)(2,1)}, bf16[2048,924]{0,1:T(8,128)(2,1)}, bf16[2048,924]{0,1:T(8,128)(2,1)}) async-done(((bf16[2048,924]{0,1:T(8,128)(2,1)}, bf16[2048,924]{0,1:T(8,128)(2,1)}, bf16[2048,924]{0,1:T(8,128)(2,1)}), (bf16[2048,924]{0,1:T(8,128)(2,1)}, bf16[2048,924]{0,1:T(8,128)(2,1)}, bf16[2048,924]{0,1:T(8,128)(2,1)})) %all-reduce.3.cloned.1.call-update) | async-done | bytes 11354128 | tf_op jit(solution)/shard_map/psum | solution.py:123
  932.6 7.3 fusion
  939.9 3.1 convolution_convert_fusion.3
  943.0 2.4 fusion.26
  945.5 3.9 add_convert_fusion
  949.4 4.5 all-to-all-start.1
  953.9 6.0 convolution_convert_fusion.4
  959.9 3.5 fusion.11
  963.4 19.8 %all-to-all-done.1 = bf16[16,128,512]{2,1,0:T(8,128)(2,1)S(1)} async-done(((bf16[16,128,512]{2,1,0:T(8,128)(2,1)}), bf16[16,128,512]{2,1,0:T(8,128)(2,1)S(1)}, u32[]{:S(2)}, u32[]{:S(2)}) %all-to-all-start.1) | async-done | bytes 2097184 | tf_op jit(solution)/shard_map/all_to_all | solution.py:40
  983.2 1.0 reduce_sum.78
  (55 shorter events, 1.9 us)
Async XLA Ops:
  7.2 455.9 %copy-start = (bf16[512,924]{0,1:T(8,128)(2,1)S(1)}, bf16[512,924]{0,1:T(8,128)(2,1)}, u32[]{:S(2)}) copy-start(bf16[512,924]{0,1:T(8,128)(2,1)} %param.17) | copy-start | bytes 2838532
  7.2 422.2 %all-gather.3.cloned.1.call-start = ((), (), s32[]{:S(2)}) async-start(), calls=%async_computation.2 | async-start | bytes 11698176 | tf_op jit(solution)/shard_map/all_gather | solution.py:28
  342.4 590.2 %all-reduce.3.cloned.1.call-start = ((), (), s32[]{:S(2)}) async-start(), calls=%async_computation.3 | async-start | bytes 22806528 | tf_op jit(solution)/shard_map/psum | solution.py:123
  449.8 23.0 %copy-start.5 = (bf16[2048,512]{1,0:T(8,128)(2,1)}, bf16[2048,512]{1,0:T(8,128)(2,1)S(1)}, u32[]{:S(2)}) copy-start(bf16[2048,512]{1,0:T(8,128)(2,1)S(1)} %gather_fusion) | copy-start | bytes 6291460
  463.0 5.9 copy-start.7
  463.0 5.9 copy-start.10
  468.9 3.9 copy-start.9
  932.6 7.3 copy-start.8
  939.9 3.2 copy-start.4
  943.0 2.4 copy-start.11
  949.4 33.8 %all-to-all-start.1 = ((bf16[16,128,512]{2,1,0:T(8,128)(2,1)}), bf16[16,128,512]{2,1,0:T(8,128)(2,1)S(1)}, u32[]{:S(2)}, u32[]{:S(2)}) async-start(bf16[16,128,512]{2,1,0:T(8,128)(2,1)} %bitcast.58), calls=%async_computation.1 | async-start | bytes 4194304 | tf_op jit(solution)/shard_map/all_to_all | solution.py:40
  953.9 6.0 copy-start.2
  953.9 6.0 copy-start.3
  953.9 6.0 copy-start.6
  959.9 24.2 %copy-start.1 = (bf16[512,924]{0,1:T(8,128)(2,1)S(1)}, bf16[512,924]{0,1:T(8,128)(2,1)}, u32[]{:S(2)}) copy-start(bf16[512,924]{0,1:T(8,128)(2,1)} %param.17) | copy-start | bytes 2838532
Sparse Core Ops, SparseCore 0:
  342.5 86.7 all-gather.2
  476.8 455.7 all-reduce.2
where the time goes:
time: 991 us
  waiting for transfers between devices  542 us (55%)
  blocking collectives  327 us (33%)
  local copies, waits for them, and re-layouts  57.6 us (6%)
  matrix products  32.5 us (3%)
  between operations  17 us (2%)
  other arithmetic  11 us (1%)
    psum x1, waiting for transfers between devices, per_device(): lax.psum(up_term.astype(jnp.bfloat16), 'col').astype(jnp.float32)  456 us
    all_gather x1, blocking collectives, per_device(): table = lax.all_gather(local, ('row', 'col'), axis=0, tiled=True)  307 us
    all_gather x1, waiting for transfers between devices, sent_together(): result = lax.all_gather(both, axis, axis=dim, tiled=True)  65.8 us
    scatter x1, local copies, waits for them, and re-layouts, source_index(): empty.at[target.reshape(-1)].set(flat_source.reshape(-1), mode='drop')  20.4 us
  transfers between devices with their start and end apart: 3, of which 3 were waited for; matrix products, arithmetic and copies ran while one was open for 3% of the time, Pallas kernels for 0%

commit v1 on v0

--- a/solution.py
+++ b/solution.py
@@ -96,7 +96,10 @@
         ],
         axis=1,
     )
-    table = lax.all_gather(local, ("row", "col"), axis=0, tiled=True)
+    table = jnp.concatenate(
+        lax.all_to_all(jnp.stack([local] * lax.axis_size(("row", "col"))), ("row", "col"), 0, 0),
+        axis=0,
+    )
     all_lengths = table[:, 0].astype(jnp.int32)
     all_owners = table[:, 1].astype(jnp.int32)
     all_prompts = table[:, 2].astype(jnp.int32)

time: 991 us -> 699 us (0.71)
  blocking collectives: 327 us -> 14.9 us
  starting transfers between devices: 4.6 us -> 15.1 us
    all_gather x1 -> x0, blocking collectives: 307 us -> none  [per_device(): table = lax.all_gather(local, ('row', 'col'), axis=0, tiled=True)]
    all_to_all x0 -> x1, starting transfers between devices: none -> 10.5 us  [per_device(): lax.all_to_all(jnp.stack([local] * lax.axis_size(('row', 'col'))), ('row'...]
  transfers between devices with their start and end apart: 3 -> 4, of which waited for: 3 -> 4; matrix products, arithmetic and copies ran while one was open for 3% -> 5% of each run, Pallas kernels for 0% -> 0%
where the time goes in v1:
time: 699 us
  waiting for transfers between devices  550 us (79%)
  local copies, waits for them, and re-layouts  58.3 us (8%)
  matrix products  32.5 us (5%)
  between operations  17 us (2%)
  starting transfers between devices  15.1 us (2%)
  blocking collectives  14.9 us (2%)
  other arithmetic  11 us (2%)
    psum x1, waiting for transfers between devices, per_device(): lax.psum(up_term.astype(jnp.bfloat16), 'col').astype(jnp.float32)  456 us
    all_gather x1, waiting for transfers between devices, sent_together(): result = lax.all_gather(both, axis, axis=dim, tiled=True)  67.7 us
    scatter x1, local copies, waits for them, and re-layouts, source_index(): empty.at[target.reshape(-1)].set(flat_source.reshape(-1), mode='drop')  20.4 us
    all_to_all x1, waiting for transfers between devices, sent_and_summed(): tiles = lax.all_to_all(cut_along(array, dim, size), axis, 0, 0, tiled=True)  19.8 us
    all_to_all x1, blocking collectives, in_one_piece(): lax.all_to_all(both, axis, split_axis=split_dim, concat_axis=concat_dim,...  14.9 us
  transfers between devices with their start and end apart: 4, of which 4 were waited for; matrix products, arithmetic and copies ran while one was open for 5% of the time, Pallas kernels for 0%

profile of v1, /device:TPU:4, one launch (start us, length us, event | category | flops | bytes accessed | tf_op | source)
XLA Modules:
  0.0 698.9 jit_solution(8992971033206636793)
XLA Ops:
  10.6 10.5 %all-to-all-start = ((f32[128,1,4]{2,1,0:T(1,128)}), f32[128,1,4]{2,1,0:T(1,128)S(1)}, u32[]{:S(2)}, u32[]{:S(2)}) async-start(f32[128,1,4]{2,1,0:T(1,128)} %stack.20), calls=%async_computation | async-start | bytes 131072 | tf_op jit(solution)/shard_map/all_to_all | solution.py:100
  21.2 1.1 copy.26
  22.3 6.7 all-to-all-done
  30.2 1.8 select_convert_fusion
  32.4 14.9 %all_to_all.15 = bf16[84,8,512]{2,0,1:T(8,128)(2,1)S(1)} all-to-all(bf16[84,8,512]{2,0,1:T(8,128)(2,1)S(1)} %copy.24), channel_id=1, replica_groups=mesh['row'=16,'col'=8] {'col'}, dimensions={1} | all-to-all | bytes 1376256 | tf_op jit(solution)/shard_map/all_to_all | solution.py:18
  47.3 1.1 copy.25
  49.1 20.4 %scatter_custom_fusion = s32[2048]{0:T(1024)S(1)} fusion(s32[5376]{0:T(1024)S(1)} %fusion.15, s32[5376]{0:T(1024)S(1)} %reshape.156, s32[]{:T(128)} %constant.19.clone.1), kind=kCustom, calls=%fused_computation.47 | custom fusion | bytes 8196 | tf_op jit(solution)/shard_map/scatter | solution.py:70
  69.5 67.7 %all-gather.2.cloned.1.call-done = bf16[84,128,512]{2,1,0:T(8,128)(2,1)} async-done(((bf16[84,8,512]{2,1,0:T(8,128)(2,1)}), bf16[84,128,512]{2,1,0:T(8,128)(2,1)}) %all-gather.2.cloned.1.call-update) | async-done | bytes 11010064 | tf_op jit(solution)/shard_map/all_gather | solution.py:28
  137.2 9.6 %fusion.25 = (bf16[42,128,512]{2,1,0:T(8,128)(2,1)}, bf16[42,128,512]{2,1,0:T(8,128)(2,1)}) fusion(bf16[84,128,512]{2,1,0:T(8,128)(2,1)} %all-gather.2.cloned.1.call-done), kind=kLoop, calls=%fused_computation.67 | loop fusion | bytes 22020096 | tf_op jit(solution)/shard_map/split | solution.py:29
  146.8 10.9 %gather_fusion = bf16[2048,512]{1,0:T(8,128)(2,1)S(1)} fusion(bf16[5376,512]{1,0:T(8,128)(2,1)} %bitcast.57, s32[2048]{0:T(1024)S(1)} %fusion.16), kind=kCustom, calls=%fused_computation.clone | custom fusion | bytes 4202496 | tf_op jit(solution)/shard_map/jit(_take)/gather | solution.py:119
  157.7 13.3 %gather_fusion.1 = bf16[2048,512]{1,0:T(8,128)(2,1)} fusion(bf16[5376,512]{1,0:T(8,128)(2,1)} %bitcast.56, s32[2048]{0:T(1024)S(1)} %fusion.16), kind=kCustom, calls=%fused_computation.1.clone | custom fusion | bytes 4202496 | tf_op jit(solution)/shard_map/jit(_take)/gather | solution.py:118
  171.0 5.9 convolution_convert_fusion
  176.9 3.9 convolution_convert_fusion.1
  180.7 3.8 convolution_convert_fusion.2
  184.6 455.9 %all-reduce.3.cloned.1.call-done = (bf16[2048,924]{0,1:T(8,128)(2,1)}, bf16[2048,924]{0,1:T(8,128)(2,1)}, bf16[2048,924]{0,1:T(8,128)(2,1)}) async-done(((bf16[2048,924]{0,1:T(8,128)(2,1)}, bf16[2048,924]{0,1:T(8,128)(2,1)}, bf16[2048,924]{0,1:T(8,128)(2,1)}), (bf16[2048,924]{0,1:T(8,128)(2,1)}, bf16[2048,924]{0,1:T(8,128)(2,1)}, bf16[2048,924]{0,1:T(8,128)(2,1)})) %all-reduce.3.cloned.1.call-update) | async-done | bytes 11354128 | tf_op jit(solution)/shard_map/psum | solution.py:126
  640.5 7.3 %fusion = (bf16[2048,924]{0,1:T(8,128)(2,1)S(1)}, bf16[2048,924]{0,1:T(8,128)(2,1)S(1)}) fusion(bf16[2048,924]{0,1:T(8,128)(2,1)} %get-tuple-element.8, bf16[2048,924]{0,1:T(8,128)(2,1)} %get-tuple-element.9, bf16[2048,924]{0,1:T(8,128)(2,1)} %get-tuple-element.7), kind=kLoop, calls=%fused_computation.9 | loop fusion | flops 30277632 | bytes 18923520 | tf_op jit(solution)/shard_map/convert_element_type | solution.py:137
  647.8 3.1 convolution_convert_fusion.3
  650.9 2.4 fusion.26
  653.4 3.9 add_convert_fusion
  657.2 4.5 all-to-all-start.2
  661.8 6.0 convolution_convert_fusion.4
  667.8 3.5 fusion.11
  671.3 19.8 %all-to-all-done.2 = bf16[16,128,512]{2,1,0:T(8,128)(2,1)S(1)} async-done(((bf16[16,128,512]{2,1,0:T(8,128)(2,1)}), bf16[16,128,512]{2,1,0:T(8,128)(2,1)S(1)}, u32[]{:S(2)}, u32[]{:S(2)}) %all-to-all-start.2) | async-done | bytes 2097184 | tf_op jit(solution)/shard_map/all_to_all | solution.py:40
  691.1 1.0 reduce_sum.78
  (57 shorter events, 3.2 us)
Async XLA Ops:
  7.2 163.8 %copy-start = (bf16[512,924]{0,1:T(8,128)(2,1)S(1)}, bf16[512,924]{0,1:T(8,128)(2,1)}, u32[]{:S(2)}) copy-start(bf16[512,924]{0,1:T(8,128)(2,1)} %param.17) | copy-start | bytes 2838532
  10.6 18.5 %all-to-all-start = ((f32[128,1,4]{2,1,0:T(1,128)}), f32[128,1,4]{2,1,0:T(1,128)S(1)}, u32[]{:S(2)}, u32[]{:S(2)}) async-start(f32[128,1,4]{2,1,0:T(1,128)} %stack.20), calls=%async_computation | async-start | bytes 131072 | tf_op jit(solution)/shard_map/all_to_all | solution.py:100
  21.1 116.1 %all-gather.2.cloned.1.call-start = ((), (), s32[]{:S(2)}) async-start(), calls=%async_computation.3 | async-start | bytes 11698176 | tf_op jit(solution)/shard_map/all_gather | solution.py:28
  48.4 592.1 %all-reduce.3.cloned.1.call-start = ((), (), s32[]{:S(2)}) async-start(), calls=%async_computation.4 | async-start | bytes 22806528 | tf_op jit(solution)/shard_map/psum | solution.py:126
  157.7 23.1 %copy-start.5 = (bf16[2048,512]{1,0:T(8,128)(2,1)}, bf16[2048,512]{1,0:T(8,128)(2,1)S(1)}, u32[]{:S(2)}) copy-start(bf16[2048,512]{1,0:T(8,128)(2,1)S(1)} %gather_fusion) | copy-start | bytes 6291460
  171.0 5.9 copy-start.7
  171.0 5.9 copy-start.10
  176.9 3.9 copy-start.9
  640.5 7.3 %copy-start.8 = (bf16[2048,512]{1,0:T(8,128)(2,1)S(1)}, bf16[2048,512]{1,0:T(8,128)(2,1)}, u32[]{:S(2)}) copy-start(bf16[2048,512]{1,0:T(8,128)(2,1)} %gather_fusion.1) | copy-start | bytes 6291460
  647.8 3.2 copy-start.4
  650.9 2.4 copy-start.11
  657.2 33.9 %all-to-all-start.2 = ((bf16[16,128,512]{2,1,0:T(8,128)(2,1)}), bf16[16,128,512]{2,1,0:T(8,128)(2,1)S(1)}, u32[]{:S(2)}, u32[]{:S(2)}) async-start(bf16[16,128,512]{2,1,0:T(8,128)(2,1)} %bitcast.58), calls=%async_computation.2 | async-start | bytes 4194304 | tf_op jit(solution)/shard_map/all_to_all | solution.py:40
  661.8 6.0 copy-start.2
  661.8 6.0 copy-start.3
  661.8 6.0 copy-start.6
  667.8 24.2 %copy-start.1 = (bf16[512,924]{0,1:T(8,128)(2,1)S(1)}, bf16[512,924]{0,1:T(8,128)(2,1)}, u32[]{:S(2)}) copy-start(bf16[512,924]{0,1:T(8,128)(2,1)} %param.17) | copy-start | bytes 2838532
Sparse Core Ops, SparseCore 0:
  48.5 88.6 all-gather.1
  184.7 455.7 all-reduce.2
